TPU v7x, 32 devices: a whole 2x2x4 slice. The times are simulated.
32 devices in a mesh: seq: 8 (over z, x), head: 4 (over y, core).
Axes of the slice: x: 2, y: 2, z: 4, core: 2. Of those that a mesh axis runs over, the one named last changes fastest.
Arguments:
- tokens: bfloat16 [2048, 1024], P('seq'), may hold values from -6 to 6
- queries: bfloat16 [2048, 1024], P('seq', 'head'), may hold values from -8 to 8
- key_rows: bfloat16 [2048, 1024], P('seq', 'head'), may hold values from -8 to 8
- values: bfloat16 [2048, 1024], P('seq', 'head'), may hold values from -6 to 6
- ssm_input: bfloat16 [2048, 2048], P('seq', 'head'), may hold values from -6 to 6
- write_proj: bfloat16 [2048, 128], P('seq'), may hold values from -6 to 6
- read_proj: bfloat16 [2048, 128], P('seq'), may hold values from -6 to 6
- log_decay: float32 [32, 2048], P('head', 'seq'), may hold values from -1 to 0
- attn_project: bfloat16 [1024, 1024], P('head'), may hold values from -0.1875 to 0.1875
- ssm_project: bfloat16 [2048, 1024], P('head'), may hold values from -0.125 to 0.125
- gauss_project: bfloat16 [1024, 768], replicated, may hold values from -0.1875 to 0.1875
- tile_owner: int32 [2048], P('seq'), may hold values from 0 to 3, as said below
Outputs:
- block_out: bfloat16 [2048, 1024], P(('seq', 'head'))
- tile_rows: bfloat16 [8, 4, 4, 32, 768], P('seq', 'head')
Inputs may be any that keep to these rules, and one draw needn't show every extreme that they name: `tile_owner`: in each aligned group of 64 tokens no owner is named by more than 32 tokens; in every block of 256 tokens one owner is named by exactly 32 tokens of each of its groups.
All inputs are finite; a program needn't handle non-finite values.
Results may differ from a plain program's by a relative error of at most 0.023.
Values may be sent and summed in bfloat16 or wider, within the bound.
A program may use at most 128 MiB of HBM per device.

v0:
```python
import math

import jax
import jax.numpy as jnp
from jax import lax
from jax.sharding import PartitionSpec as P

HDIM = 64


def entering_2(array, axis, combine, identity):
    devices, mine = (lax.axis_size(axis), lax.axis_index(axis))
    everything = jax.tree.map(
        lambda part, kind: lax.all_gather(part.astype(kind), axis),
        array,
        (jnp.bfloat16, jnp.bfloat16),
    )
    start = jax.tree.map(
        lambda part, zero: jnp.broadcast_to(jnp.asarray(zero, part.dtype), part.shape),
        array,
        identity,
    )

    def hop(k, before):
        reached = k < mine
        new = combine(
            before, jax.tree.map(lambda part, own: part[k].astype(own.dtype), everything, array)
        )
        return jax.tree.map(lambda a, b: jnp.where(reached, a, b), new, before)

    return lax.fori_loop(0, devices, hop, start)


def chain_pieces(ssm_input, write_proj, read_proj, log_decay):
    row_count = write_proj.shape[0]
    head_count = log_decay.shape[0]
    head_width = ssm_input.shape[1] // head_count
    cumulative = jnp.cumsum(log_decay, axis=1)
    inputs_heads = ssm_input.reshape(row_count, head_count, head_width)
    later_rows = lax.broadcasted_iota(jnp.int32, (row_count, row_count), 0)
    earlier_cols = lax.broadcasted_iota(jnp.int32, (row_count, row_count), 1)
    log_gaps = cumulative[:, :, None] - cumulative[:, None, :]
    decays = jnp.exp(jnp.where((later_rows >= earlier_cols)[None], log_gaps, -jnp.inf))
    cross_terms = jnp.dot(read_proj, write_proj.T, preferred_element_type=jnp.float32)
    mixing = (decays * cross_terms[None]).astype(jnp.bfloat16)
    inner_part = jnp.einsum(
        "hts,shp->thp", mixing, inputs_heads, preferred_element_type=jnp.float32
    )
    tail_decay = jnp.exp(cumulative[:, -1:] - cumulative)
    tail_inputs = (inputs_heads.astype(jnp.float32) * tail_decay.T[:, :, None]).astype(jnp.bfloat16)
    local_state = jnp.einsum(
        "sn,shp->hnp", write_proj, tail_inputs, preferred_element_type=jnp.float32
    )
    total_decay = jnp.exp(cumulative[:, -1])
    return (cumulative, inner_part, local_state, total_decay)


def chain_output(cumulative, inner_part, entering, read_proj):
    entering_low = entering.astype(jnp.bfloat16)
    outer_part = jnp.einsum(
        "tn,hnp->thp", read_proj, entering_low, preferred_element_type=jnp.float32
    )
    mixture = inner_part + outer_part * jnp.exp(cumulative).T[:, :, None]
    scaled = mixture * lax.rsqrt(jnp.mean(mixture * mixture, axis=2, keepdims=True) + 1e-05)
    return scaled.reshape(scaled.shape[0], -1).astype(jnp.bfloat16)


def combine_states(earlier, latter):
    decay_first, state_first = earlier
    decay_second, state_second = latter
    return (decay_first * decay_second, decay_second[:, None, None] * state_first + state_second)


def pass_states(local_state, total_decay):
    identity = (jnp.ones_like(total_decay), jnp.zeros_like(local_state))
    prefix = entering_2((total_decay, local_state), "seq", combine_states, identity)
    return prefix[1]


def fold_keys(query_heads, key_rows, values):
    row_count, head_count, head_width = query_heads.shape
    scale = 1.0 / math.sqrt(head_width)
    initial = (
        jnp.full((head_count, row_count), -jnp.inf, jnp.float32),
        jnp.zeros((head_count, row_count), jnp.float32),
        jnp.zeros((head_count, row_count, head_width), jnp.float32),
    )
    key_piece = lax.all_gather(key_rows, "seq", axis=0, tiled=True)
    value_piece = lax.all_gather(values, "seq", axis=0, tiled=True)
    piece_rows = key_piece.shape[0]
    block_rows = math.gcd(piece_rows, 1024)

    def one_step(block_index, carry_state):
        run_max, run_sum, accumulated = carry_state
        key_block = lax.dynamic_slice_in_dim(
            key_piece, block_index * block_rows, block_rows, 0
        ).reshape(block_rows, head_count, head_width)
        value_block = lax.dynamic_slice_in_dim(
            value_piece, block_index * block_rows, block_rows, 0
        ).reshape(block_rows, head_count, head_width)
        scores = (
            jnp.einsum("qhd,khd->hqk", query_heads, key_block, preferred_element_type=jnp.float32)
            * scale
        )
        new_max = jnp.maximum(run_max, jnp.max(scores, axis=2))
        shrink = jnp.exp(run_max - new_max)
        raised = jnp.exp(scores - new_max[:, :, None])
        run_sum = run_sum * shrink + jnp.sum(raised, axis=2)
        accumulated = accumulated * shrink[:, :, None] + jnp.einsum(
            "hqk,khd->hqd",
            raised.astype(jnp.bfloat16),
            value_block,
            preferred_element_type=jnp.float32,
        )
        return (new_max, run_sum, accumulated)

    run_max, run_sum, accumulated = lax.fori_loop(0, piece_rows // block_rows, one_step, initial)
    attended = accumulated / run_sum[:, :, None]
    return (
        attended.transpose(1, 0, 2).reshape(row_count, head_count * head_width).astype(jnp.bfloat16)
    )


def slot_rank(owners_here, owner_count, group_rows):
    row_count = owners_here.shape[0]
    one_hot = (owners_here[:, None] == jnp.arange(owner_count, dtype=jnp.int32)[None, :]).astype(
        jnp.bfloat16
    )
    later_rows = lax.broadcasted_iota(jnp.int32, (row_count, row_count), 0)
    earlier_cols = lax.broadcasted_iota(jnp.int32, (row_count, row_count), 1)
    before = (
        (earlier_cols < later_rows) & (later_rows // group_rows == earlier_cols // group_rows)
    ).astype(jnp.bfloat16)
    counted = jnp.dot(before, one_hot, preferred_element_type=jnp.float32)
    return jnp.sum(counted * one_hot.astype(jnp.float32), axis=1)


def per_device(
    tokens,
    queries,
    key_rows,
    values,
    ssm_input,
    write_proj,
    read_proj,
    log_decay,
    attn_project,
    ssm_project,
    gauss_project,
    tile_owner,
):
    row_count = queries.shape[0]
    head_count = queries.shape[1] // HDIM
    query_heads = queries.reshape(row_count, head_count, HDIM)
    attended = fold_keys(query_heads, key_rows, values)
    cumulative, inner_part, local_state, total_decay = chain_pieces(
        ssm_input, write_proj, read_proj, log_decay
    )
    entering = pass_states(local_state, total_decay)
    ssm_mix = chain_output(cumulative, inner_part, entering, read_proj)
    owner_count = lax.axis_size("head")
    own_index = lax.axis_index("head")
    sub_rows = row_count // owner_count
    capacity = sub_rows // 2
    width_out = gauss_project.shape[1]
    slot_count = owner_count * capacity
    slot_ids = jnp.arange(slot_count, dtype=jnp.float32)
    update = lax.psum_scatter(
        (
            jnp.dot(attended, attn_project, preferred_element_type=jnp.float32)
            + jnp.dot(ssm_mix, ssm_project, preferred_element_type=jnp.float32)
        ).astype(jnp.bfloat16),
        "head",
        scatter_dimension=0,
        tiled=True,
    ).astype(jnp.float32)
    own_tokens = lax.dynamic_slice_in_dim(tokens, own_index * sub_rows, sub_rows, 0)
    block_out = (own_tokens.astype(jnp.float32) + update).astype(jnp.bfloat16)
    gaussians = jnp.dot(block_out, gauss_project, preferred_element_type=jnp.float32).astype(
        jnp.bfloat16
    )
    owners_here = lax.dynamic_slice_in_dim(tile_owner, own_index * sub_rows, sub_rows, 0)
    slot_value = owners_here.astype(jnp.float32) * capacity + slot_rank(
        owners_here, owner_count, sub_rows
    )
    selector = (slot_ids[:, None] == slot_value[None, :]).astype(jnp.bfloat16)
    packed = jnp.dot(selector, gaussians, preferred_element_type=jnp.float32).astype(jnp.bfloat16)
    packed = packed.reshape(owner_count, capacity, width_out)
    received = lax.all_to_all(packed, "head", split_axis=0, concat_axis=0, tiled=True)
    tile_rows = received.reshape(1, 1, owner_count, capacity, width_out)
    return (block_out, tile_rows)


def solution(mesh):
    in_specs = (
        P("seq", None),
        P("seq", "head"),
        P("seq", "head"),
        P("seq", "head"),
        P("seq", "head"),
        P("seq", None),
        P("seq", None),
        P("head", "seq"),
        P("head", None),
        P("head", None),
        P(),
        P("seq"),
    )
    out_specs = (P(("seq", "head"), None), P("seq", "head", None, None, None))
    return jax.shard_map(
        per_device, mesh=mesh, in_specs=in_specs, out_specs=out_specs, check_vma=False
    )
```

profile of v0, /device:TPU:0, one launch (start us, length us, event | category | flops | bytes accessed | tf_op | source)
XLA Modules:
  0.0 194.4 jit_solution(14442485503566040951)
XLA Ops:
  7.2 1.4 reduce-window.6
  9.1 1.1 copy.44
  10.2 1.7 fusion.16
  12.0 1.7 copy.41
  13.8 1.7 copy.43
  16.3 1.2 dynamic-slice
  18.4 23.1 %all-reduce = bf16[64]{0:T(256)(128)(2,1)S(1)} all-reduce(bf16[64]{0:T(256)(128)(2,1)S(1)} %dynamic-update-slice), channel_id=2, replica_groups=mesh['seq'=8,'head'=4] {'seq'}, use_global_device_ids=true, to_apply=%add | all-reduce | flops 64 | bytes 256
  41.6 1.1 fusion.40
  42.7 1.0 copy.42
  43.7 11.2 %all-gather.10.cloned.1.call-done = bf16[64,128,64]{1,2,0:T(8,128)(2,1)} async-done(((bf16[8,128,64]{1,2,0:T(8,128)(2,1)}), bf16[64,128,64]{1,2,0:T(8,128)(2,1)}) %all-gather.10.cloned.1.call-update) | async-done | bytes 1048592 | tf_op jit(solution)/shard_map/all_gather | solution.py:14
  54.9 10.3 %while.33 = (s32[]{:T(128)}, f32[8,128,64]{2,1,0:T(8,128)S(1)}, s32[]{:T(128)}, bf16[8,8]{1,0:T(8,128)(2,1)S(1)}, bf16[8,8,128,64]{2,3,1,0:T(8,128)(2,1)}, /*index=5*/s32[]{:T(128)}, s32[]{:T(128)}) while((s32[]{:T(128)}, f32[8,128,64]{2,1,0:T(8,128)S(1)}, s32[]{:T(128)}, bf16[8,8]{1,0:T(8,128)(2,1)S(1)}, ...), condition=%wide.region_7.8_spmd.clone, body=%wide.region_6.7_spmd.clone.sunk | while | flops 327692 | bytes 1179833 | solution.py:31
  54.9 0.9 constant_dynamic-slice_fusion.6
  56.2 0.9 constant_dynamic-slice_fusion.6
  57.5 0.9 constant_dynamic-slice_fusion.6
  62.7 0.9 constant_dynamic-slice_fusion.6
  64.0 0.9 constant_dynamic-slice_fusion.6
  65.5 2.4 %multiply_reduce_fusion = (f32[256,8]{0,1:T(8,128)S(1)}, f32[256,8,64]{0,2,1:T(8,128)}) fusion(f32[256,8,64]{0,2,1:T(8,128)S(1)} %fusion.15, bf16[256,8,64]{0,2,1:T(8,128)(2,1)S(1)} %bitcast.91, f32[256,256]{1,0:T(8,128)S(1)} %fusion.40, f32[8,256]{1,0:T(8,128)S(1)} %get-tuple-element.313, pred[256,256]{1,0:T(8,128)(4,1)} %iota_compare_fusion), kind=kOutput, calls=%fused_computation.40 | convolution fusion | flops 69597184 | bytes 1654784 | tf_op jit(solution)/shard_map/hts,shp->thp/dot_general | solution.py:46
  67.9 28.1 %all-gather.6.cloned.1.call-done = bf16[2048,256]{0,1:T(8,128)(2,1)} async-done(((bf16[256,256]{0,1:T(8,128)(2,1)}), bf16[2048,256]{0,1:T(8,128)(2,1)}) %all-gather.6.cloned.1.call-update) | async-done | bytes 1048592 | tf_op jit(solution)/shard_map/all_gather | solution.py:88
  96.0 40.5 %all-gather.8.cloned.1.call-done = bf16[2048,256]{0,1:T(8,128)(2,1)} async-done(((bf16[256,256]{0,1:T(8,128)(2,1)}), bf16[2048,256]{0,1:T(8,128)(2,1)}) %all-gather.8.cloned.1.call-update) | async-done | bytes 1048592 | tf_op jit(solution)/shard_map/all_gather | solution.py:89
  136.5 16.7 %while.32 = (s32[]{:T(128)}, f32[4,256]{1,0:T(4,128)S(1)}, f32[4,256]{1,0:T(4,128)S(1)}, f32[4,256,64]{1,2,0:T(8,128)S(1)}, bf16[2048,256]{0,1:T(8,128)(2,1)}, /...) while((s32[]{:T(128)}, f32[4,256]{1,0:T(4,128)S(1)}, ...), condition=%wide.region_3.0_spmd.clone, body=%wide.region_0.0_spmd.clone.sunk | while | flops 277025792 | bytes 33226948 | solution.py:117
  136.5 1.3 constant_dynamic-slice_fusion.5
  137.8 2.7 %bitcast_reduce_fusion.2 = (f32[4,256]{1,0:T(4,128)S(1)}, f32[4,1024,256]{2,1,0:T(8,128)}) fusion(bf16[1024,4,64]{0,2,1:T(8,128)(2,1)S(1)} %bitcast.87, bf16[256,4,64]{0,2,1:T(8,128)(2,1)S(1)} %get-tuple-element.456), kind=kOutput, calls=%fused_computation.1.clone.1 | convolution fusion | flops 136313856 | bytes 4853760 | tf_op jit(solution)/shard_map/while/body/eval_jaxpr/qhd,khd->hqk/dot_general | solution.py:102
  140.5 3.0 %fusion.66 = f32[4,256]{1,0:T(4,128)S(1)} fusion(f32[4,1024,256]{2,1,0:T(8,128)} %get-tuple-element.399, f32[4,256]{1,0:T(4,128)S(1)} %select_maximum_fusion.2), kind=kLoop, calls=%fused_computation.4.clone.1 | loop fusion | flops 3144704 | bytes 4202496 | tf_op jit(solution)/shard_map/while/body/eval_jaxpr/reduce_sum | solution.py:108
  144.8 1.3 constant_dynamic-slice_fusion.5
  146.1 2.7 %bitcast_reduce_fusion.2 = (f32[4,256]{1,0:T(4,128)S(1)}, f32[4,1024,256]{2,1,0:T(8,128)}) fusion(bf16[1024,4,64]{0,2,1:T(8,128)(2,1)S(1)} %bitcast.87, bf16[256,4,64]{0,2,1:T(8,128)(2,1)S(1)} %get-tuple-element.456), kind=kOutput, calls=%fused_computation.1.clone.1 | convolution fusion | flops 136313856 | bytes 4853760 | tf_op jit(solution)/shard_map/while/body/eval_jaxpr/qhd,khd->hqk/dot_general | solution.py:102
  148.8 3.0 %fusion.66 = f32[4,256]{1,0:T(4,128)S(1)} fusion(f32[4,1024,256]{2,1,0:T(8,128)} %get-tuple-element.399, f32[4,256]{1,0:T(4,128)S(1)} %select_maximum_fusion.2), kind=kLoop, calls=%fused_computation.4.clone.1 | loop fusion | flops 3144704 | bytes 4202496 | tf_op jit(solution)/shard_map/while/body/eval_jaxpr/reduce_sum | solution.py:108
  153.2 1.1 multiply_convert_fusion.2
  154.3 1.7 fusion.41
  156.0 1.1 fusion.13
  157.6 20.3 %reduce-scatter.2.cloned.1.call-done = bf16[64,1024]{1,0:T(8,128)(2,1)} async-done(((bf16[256,1024]{1,0:T(8,128)(2,1)}), bf16[64,1024]{1,0:T(8,128)(2,1)}) %reduce-scatter.2.cloned.1.call-update) | async-done | bytes 131088 | tf_op jit(solution)/shard_map/reduce_scatter | solution.py:168
  177.9 1.0 add_convert_fusion
  179.5 7.7 %all_to_all.5 = bf16[4,32,768]{2,1,0:T(8,128)(2,1)S(1)} all-to-all(bf16[4,32,768]{2,1,0:T(8,128)(2,1)S(1)} %bitcast.92), channel_id=1, replica_groups=mesh['seq'=8,'head'=4] {'head'}, dimensions={0} | all-to-all | bytes 393216 | tf_op jit(solution)/shard_map/all_to_all | solution.py:189
  (82 shorter events, 11.9 us)
Async XLA Ops:
  7.2 171.7 %copy-start = (bf16[1024,768]{1,0:T(8,128)(2,1)S(1)}, bf16[1024,768]{1,0:T(8,128)(2,1)}, u32[]{:S(2)}) copy-start(bf16[1024,768]{1,0:T(8,128)(2,1)} %param.26) | copy-start | bytes 4718596
  7.2 47.7 %all-gather.10.cloned.1.call-start = ((), (), s32[]{:S(2)}) async-start(), calls=%async_computation.5 | async-start | bytes 1179648 | tf_op jit(solution)/shard_map/all_gather | solution.py:14
  12.0 84.0 %all-gather.6.cloned.1.call-start = ((), (), s32[]{:S(2)}) async-start(), calls=%async_computation.2 | async-start | bytes 1179648 | tf_op jit(solution)/shard_map/all_gather | solution.py:88
  13.7 122.7 %all-gather.8.cloned.1.call-start = ((), (), s32[]{:S(2)}) async-start(), calls=%async_computation.3 | async-start | bytes 1179648 | tf_op jit(solution)/shard_map/all_gather | solution.py:89
  15.5 162.4 %reduce-scatter.2.cloned.1.call-start = ((), (), s32[]{:S(2)}) async-start(), calls=%async_computation.4 | async-start | bytes 655360 | tf_op jit(solution)/shard_map/reduce_scatter | solution.py:168
  54.9 10.3 %copy-start.4 = (bf16[256,128]{1,0:T(8,128)(2,1)S(1)}, bf16[256,128]{1,0:T(8,128)(2,1)}, u32[]{:S(2)}) copy-start(bf16[256,128]{1,0:T(8,128)(2,1)} %param.22) | copy-start | bytes 196612
  136.5 19.5 %copy-start.2 = (bf16[256,1024]{1,0:T(8,128)(2,1)S(1)}, bf16[256,1024]{1,0:T(8,128)(2,1)}, u32[]{:S(2)}) copy-start(bf16[256,1024]{1,0:T(8,128)(2,1)} %param.24) | copy-start | bytes 1572868
  140.5 3.4 %copy-start.1 = (f32[4,1024,256]{2,1,0:T(8,128)S(1)}, f32[4,1024,256]{2,1,0:T(8,128)}, u32[]{:S(2)}) copy-start(f32[4,1024,256]{2,1,0:T(8,128)} %get-tuple-element.399) | copy-start | bytes 12582916 | tf_op jit(solution)/shard_map/while
  148.8 3.4 %copy-start.1 = (f32[4,1024,256]{2,1,0:T(8,128)S(1)}, f32[4,1024,256]{2,1,0:T(8,128)}, u32[]{:S(2)}) copy-start(f32[4,1024,256]{2,1,0:T(8,128)} %get-tuple-element.399) | copy-start | bytes 12582916 | tf_op jit(solution)/shard_map/while
  153.2 4.0 %copy-start.5 = (s32[256]{0:T(256)S(1)}, s32[256]{0:T(256)}, u32[]{:S(2)}) copy-start(s32[256]{0:T(256)} %param.27) | copy-start | bytes 3076
  178.9 9.0 %copy-start.3 = (bf16[64,1024]{1,0:T(8,128)(2,1)}, bf16[64,1024]{1,0:T(8,128)(2,1)S(1)}, u32[]{:S(2)}) copy-start(bf16[64,1024]{1,0:T(8,128)(2,1)S(1)} %add_convert_fusion) | copy-start | bytes 393220
Sparse Core Ops, SparseCore 0:
  12.1 42.7 all-gather.9
  57.5 38.3 all-gather.5
  98.0 38.4 all-gather.7
  157.3 20.5 reduce-scatter.1
where the time goes:
time: 195 us; the launch traced here: 194 us
  waiting for transfers between devices  100 us (51%)
  blocking collectives  30.8 us (16%)
  local copies, waits for them, and re-layouts  20.3 us (10%)
  matrix products  16.2 us (8%)
  between operations  14.5 us (7%)
  other arithmetic  11.9 us (6%)
    all_gather x1, waiting for transfers between devices, fold_keys(): value_piece = lax.all_gather(values, 'seq', axis=0, tiled=True)  40.5 us
    all_gather x1, waiting for transfers between devices, fold_keys(): key_piece = lax.all_gather(key_rows, 'seq', axis=0, tiled=True)  28.1 us
    unnamed x1, blocking collectives  23.1 us
    reduce_scatter x1, waiting for transfers between devices, per_device(): lax.psum_scatter((jnp.dot(attended, attn_project, preferred_element_type=...  20.3 us
    all_gather x1, waiting for transfers between devices, entering_2(): lax.all_gather(part.astype(kind), axis)  11.2 us
    dynamic_slice x16, local copies, waits for them, and re-layouts, hop(): part[k].astype(own.dtype)  8.8 us
    all_to_all x1, blocking collectives, per_device(): lax.all_to_all(packed, 'head', split_axis=0, concat_axis=0, tiled=True)  7.7 us
    unnamed x18, local copies, waits for them, and re-layouts  7.62 us
  transfers between devices with their start and end apart: 4, of which 4 were waited for; matrix products, arithmetic and copies ran while one was open for 11% of the time, Pallas kernels for 0%

commit v1 on v0

v1 whole, which is shorter than its diff:
```python
import functools
import math

import jax
import jax.numpy as jnp
from jax import lax
from jax.experimental import pallas as pl
from jax.experimental.pallas import tpu as pltpu
from jax.sharding import PartitionSpec as P

HDIM = 64
F32 = jnp.float32
BF16 = jnp.bfloat16
MESH = pl.DeviceIdType.MESH


def partner(index, step):
    out = index
    bit = 1
    while bit <= step:
        if step & bit:
            out = out + bit - 2 * bit * ((index // bit) % 2)
        bit *= 2
    return out


def dot(a, b):
    return jnp.dot(a, b, preferred_element_type=F32)


def dot_nt(a, b):
    return lax.dot_general(a, b, (((1,), (1,)), ((), ())), preferred_element_type=F32)


def dot_tn(a, b):
    return lax.dot_general(a, b, (((0,), (0,)), ((), ())), preferred_element_type=F32)


def kernel(
    seq,
    owners,
    tokens_hbm,
    queries_hbm,
    keys_hbm,
    values_hbm,
    ssm_hbm,
    write_hbm,
    read_hbm,
    decay_hbm,
    attn_w_hbm,
    ssm_w_hbm,
    gauss_w_hbm,
    owner_ref,
    block_out,
    tiles_out,
    tokens_v,
    queries_v,
    keys_v,
    values_v,
    ssm_v,
    write_v,
    read_v,
    decay_v,
    attn_w,
    ssm_w,
    gauss_w,
    kv_out,
    q_out,
    kv_in,
    q_in,
    st_out,
    st_in,
    en_out,
    en_in,
    acc,
    top,
    o_out,
    mix,
    inner,
    upd,
    up_out,
    up_in,
    pk_out,
    load_sem,
    kv_ss,
    kv_rs,
    q_ss,
    q_rs,
    fw_ss,
    fw_rs,
    st_ss,
    st_rs,
    en_ss,
    en_rs,
    o_ss,
    o_rs,
    up_ss,
    up_rs,
    tl_ss,
    tl_rs,
):
    me = lax.axis_index("seq")
    own = lax.axis_index("head")
    rows = queries_v.shape[0]
    heads = queries_v.shape[1] // HDIM
    members = seq // heads
    my_head = me // members
    my_group = me % members
    ssm_heads = decay_v.shape[0]
    width = ssm_v.shape[1] // ssm_heads
    part = st_in.shape[1] - 16
    sub = rows // owners
    cap = sub // 2

    def remote(src, dst, send, recv, target):
        return pltpu.make_async_remote_copy(
            src_ref=src, dst_ref=dst, send_sem=send, recv_sem=recv,
            device_id=target, device_id_type=MESH,
        )

    sources = [
        (queries_hbm, queries_v),
        (keys_hbm, keys_v),
        (values_hbm, values_v),
        (decay_hbm, decay_v),
        (ssm_hbm, ssm_v),
        (write_hbm, write_v),
        (read_hbm, read_v),
        (ssm_w_hbm, ssm_w),
        (attn_w_hbm, attn_w),
        (tokens_hbm.at[pl.ds(own * sub, sub)], tokens_v),
        (gauss_w_hbm, gauss_w),
    ]
    loads = [pltpu.make_async_copy(a, b, load_sem.at[i]) for i, (a, b) in enumerate(sources)]
    for load in loads:
        load.start()

    barrier = pltpu.get_barrier_semaphore()
    for r in range(1, seq):
        pl.semaphore_signal(barrier, inc=1, device_id={"seq": (me + r) % seq}, device_id_type=MESH)
    for r in range(1, owners):
        pl.semaphore_signal(
            barrier, inc=1, device_id={"head": (own + r) % owners}, device_id_type=MESH
        )

    loads[0].wait()
    q_t = (queries_v[...].astype(F32) * (1.0 / math.sqrt(HDIM))).astype(BF16).T
    for h in range(heads):
        q_out[h] = q_t[h * HDIM : (h + 1) * HDIM]
    loads[1].wait()
    loads[2].wait()
    for h in range(heads):
        cols = slice(h * HDIM, (h + 1) * HDIM)
        kv_out[h] = jnp.concatenate([keys_v[:, cols], values_v[:, cols]], axis=1)
    pl.semaphore_wait(barrier, seq - 1 + owners - 1)

    q_copies, kv_copies = [], []
    for r in range(1, heads):
        j = partner(my_head, r)
        target = {"seq": j * members + my_group}
        q_copies.append(remote(q_out.at[j], q_in.at[my_head], q_ss.at[r], q_rs.at[r], target))
        kv_copies.append(remote(kv_out.at[j], kv_in.at[me], kv_ss.at[r], kv_rs.at[r], target))

    def forward(r):
        slot = partner(my_head, r) * members + my_group
        source = kv_in.at[slot] if r else kv_out.at[my_head]
        copies = []
        for m in range(1, members):
            target = {"seq": my_head * members + (my_group + m) % members}
            copies.append(
                remote(source, kv_in.at[slot], fw_ss.at[r, m], fw_rs.at[r, m], target)
            )
        for copy in copies:
            copy.start()
        return copies

    for copy in q_copies:
        copy.start()
    forwards = {0: forward(0)}
    for copy in kv_copies:
        copy.start()
    q_in[my_head] = q_out[my_head]
    kv_in[me] = kv_out[my_head]

    loads[3].wait()
    log_decay = decay_v[...]
    high = log_decay.astype(BF16)
    rest = log_decay - high.astype(F32)
    middle = rest.astype(BF16)
    low = (rest - middle.astype(F32)).astype(BF16)
    s_index = lax.broadcasted_iota(jnp.int32, (rows, rows), 0)
    t_index = lax.broadcasted_iota(jnp.int32, (rows, rows), 1)
    causal = s_index <= t_index
    upto = jnp.where(causal, 1.0, 0.0).astype(BF16)
    cumulative = dot(high, upto) + dot(middle, upto) + dot(low, upto)
    block_end = cumulative[:, rows - 1 : rows]
    total = jnp.exp(block_end)
    loads[4].wait()
    loads[5].wait()
    ssm_t = ssm_v[...].T
    tail_decay = jnp.exp(block_end - cumulative)
    tails = jnp.concatenate(
        [
            (ssm_t[g * width : (g + 1) * width].astype(F32) * tail_decay[g : g + 1]).astype(BF16)
            for g in range(ssm_heads)
        ],
        axis=0,
    )
    local = dot(tails, write_v[...])
    for d in range(seq):
        g = d * part // width
        decay_rows = jnp.broadcast_to(total[g : g + 1], (8, local.shape[1]))
        decay_rest = decay_rows - decay_rows.astype(BF16).astype(F32)
        st_out[d] = jnp.concatenate(
            [local[d * part : (d + 1) * part], decay_rows, decay_rest], axis=0
        ).astype(BF16)
    st_copies = []
    for r in range(1, seq):
        d = (me + r) % seq
        st_copies.append(
            remote(st_out.at[d], st_in.at[me], st_ss.at[r], st_rs.at[r], {"seq": d})
        )
    for copy in st_copies:
        copy.start()
    st_in[me] = st_out[me]

    loads[6].wait()
    cross = dot_nt(write_v[...], read_v[...])
    cum_cols = jnp.concatenate(
        [cumulative, jnp.zeros((128 - ssm_heads, rows), F32)], axis=0
    ).T
    for g in range(ssm_heads):
        gaps = cumulative[g : g + 1] - cum_cols[:, g : g + 1]
        mixing = (jnp.exp(jnp.where(causal, gaps, -jnp.inf)) * cross).astype(BF16)
        inner[g * width : (g + 1) * width] = dot(ssm_t[g * width : (g + 1) * width], mixing)

    for r in range(1, heads):
        kv_copies[r - 1].wait_recv()
        forwards[r] = forward(r)

    for copy in st_copies:
        copy.wait_recv()
    state = jnp.zeros((part, local.shape[1]), F32)
    for b in range(seq):
        en_out[b] = state.astype(BF16)
        if b < seq - 1:
            arrived = st_in[b].astype(F32)
            decay = arrived[part : part + 1] + arrived[part + 8 : part + 9]
            state = decay * state + arrived[:part]
    en_copies = []
    for r in range(1, seq):
        d = (me + r) % seq
        en_copies.append(
            remote(en_out.at[d], en_in.at[me], en_ss.at[r], en_rs.at[r], {"seq": d})
        )
    for copy in en_copies:
        copy.start()
    en_in[me] = en_out[me]

    for copy in q_copies:
        copy.wait_recv()
    key_rows = members * rows
    below = lax.broadcasted_iota(jnp.int32, (2 * HDIM, key_rows), 0) < HDIM
    zeros = jnp.zeros((HDIM, rows), BF16)
    for r in range(heads):
        for m in range(1, members):
            forwards[r][m - 1].wait_recv()
        a = partner(my_head, r)
        kv = kv_in[pl.ds(a * members, members)].reshape(key_rows, 2 * HDIM)
        v_t = jnp.where(below, jnp.ones((), BF16), kv.T)
        for c in range(heads):
            scores = dot(kv, jnp.concatenate([q_in[c], zeros], axis=0))
            highest = jnp.max(scores, axis=0, keepdims=True)
            if r:
                before = top[c, 0:1]
                highest = jnp.maximum(highest, before)
            weights = jnp.exp(scores - highest).astype(BF16)
            summed = dot(v_t, weights)
            if r:
                summed = summed + acc[c] * jnp.exp(before - highest)
            if r < heads - 1:
                acc[c] = summed
                top[c] = jnp.broadcast_to(highest, (8, rows))
            else:
                o_out[c] = (summed[HDIM:] / summed[0:1]).astype(BF16)
    o_copies = []
    for r in range(1, heads):
        j = partner(my_head, r)
        o_copies.append(
            remote(
                o_out.at[j], mix.at[my_head], o_ss.at[r], o_rs.at[r],
                {"seq": j * members + my_group},
            )
        )
    for copy in o_copies:
        copy.start()
    mix[my_head] = o_out[my_head]

    for copy in en_copies:
        copy.wait_recv()
    entering = en_in[...]
    if part % 16:
        entering = entering.astype(F32)
    entering = entering.reshape(seq * part, local.shape[1]).astype(BF16)
    outer = dot_nt(entering, read_v[...])
    grown = jnp.exp(cumulative)
    mixed = []
    for g in range(ssm_heads):
        span = slice(g * width, (g + 1) * width)
        out = inner[span] + outer[span] * grown[g : g + 1]
        mean = jnp.mean(out * out, axis=0, keepdims=True)
        mixed.append((out * lax.rsqrt(mean + 1e-05)).astype(BF16))
    loads[7].wait()
    upd[...] = dot_tn(jnp.concatenate(mixed, axis=0), ssm_w[...])

    named = jnp.zeros((1, sub), jnp.int32)
    for q in range(owners):
        named = jnp.where(own == q, owner_ref[:, q * sub : (q + 1) * sub], named)
    one_hot = jnp.where(
        lax.broadcasted_iota(jnp.int32, (8, sub), 0) == named, 1.0, 0.0
    )
    earlier = jnp.where(
        lax.broadcasted_iota(jnp.int32, (sub, sub), 0)
        < lax.broadcasted_iota(jnp.int32, (sub, sub), 1),
        1.0,
        0.0,
    )
    counted = dot(one_hot.astype(BF16), earlier.astype(BF16))
    rank = jnp.sum(counted * one_hot, axis=0, keepdims=True)
    slot = named * cap + rank.astype(jnp.int32)
    selector = jnp.where(
        lax.broadcasted_iota(jnp.int32, (owners * cap, sub), 0) == slot, 1.0, 0.0
    ).astype(BF16)

    loads[8].wait()
    for copy in o_copies:
        copy.wait_recv()
    attended = mix[...].reshape(heads * HDIM, rows)
    update = upd[...] + dot_tn(attended, attn_w[...])
    for q in range(owners):
        up_out[q] = update[q * sub : (q + 1) * sub].astype(BF16)
    up_copies = []
    for r in (3, 2, 1) if owners == 4 else range(1, owners):
        q = partner(own, r)
        up_copies.append(
            remote(up_out.at[q], up_in.at[r], up_ss.at[r], up_rs.at[r], {"head": q})
        )
    for copy in up_copies:
        copy.start()
    loads[9].wait()
    loads[10].wait()
    summed = up_out[own].astype(F32)
    for copy in up_copies:
        copy.wait_recv()
    for r in range(1, owners):
        summed = summed + up_in[r].astype(F32)
    block = (tokens_v[...].astype(F32) + summed).astype(BF16)
    block_out[...] = block
    gauss = dot(block, gauss_w[...]).astype(BF16)
    packed = dot(selector, gauss).astype(BF16)
    for q in range(owners):
        pk_out[q] = packed[q * cap : (q + 1) * cap]
    tl_copies = []
    for r in (3, 2, 1) if owners == 4 else range(1, owners):
        q = partner(own, r)
        tl_copies.append(
            remote(pk_out.at[q], tiles_out.at[0, 0, own], tl_ss.at[r], tl_rs.at[r], {"head": q})
        )
    for copy in tl_copies:
        copy.start()
    tiles_out[0, 0, own] = pk_out[own]
    for copy in q_copies + kv_copies + st_copies + en_copies + o_copies + up_copies:
        copy.wait_send()
    for copies in forwards.values():
        for copy in copies:
            copy.wait_send()
    for copy in tl_copies:
        copy.wait()


def per_device(seq, owners, *args):
    (tokens, queries, key_rows, values, ssm_input, write_proj, read_proj, log_decay,
     attn_project, ssm_project, gauss_project, tile_owner) = args
    rows = queries.shape[0]
    heads = queries.shape[1] // HDIM
    members = seq // heads
    model = tokens.shape[1]
    sub = rows // owners
    cap = sub // 2
    gauss_width = gauss_project.shape[1]
    channels = ssm_input.shape[1]
    state = write_proj.shape[1]
    part = channels // seq
    hbm = pl.BlockSpec(memory_space=pl.ANY)
    vmem = pl.BlockSpec(memory_space=pltpu.VMEM)
    dma = pltpu.SemaphoreType.DMA
    like = lambda a: pltpu.VMEM(a.shape, a.dtype)
    return pl.pallas_call(
        functools.partial(kernel, seq, owners),
        out_shape=(
            jax.ShapeDtypeStruct((sub, model), BF16),
            jax.ShapeDtypeStruct((1, 1, owners, cap, gauss_width), BF16),
        ),
        in_specs=[hbm] * 11 + [vmem],
        out_specs=(vmem, vmem),
        scratch_shapes=[
            pltpu.VMEM((sub, model), BF16),
            like(queries),
            like(key_rows),
            like(values),
            like(ssm_input),
            like(write_proj),
            like(read_proj),
            like(log_decay),
            like(attn_project),
            like(ssm_project),
            like(gauss_project),
            pltpu.VMEM((heads, rows, 2 * HDIM), BF16),
            pltpu.VMEM((heads, HDIM, rows), BF16),
            pltpu.VMEM((seq, rows, 2 * HDIM), BF16),
            pltpu.VMEM((heads, HDIM, rows), BF16),
            pltpu.VMEM((seq, part + 16, state), BF16),
            pltpu.VMEM((seq, part + 16, state), BF16),
            pltpu.VMEM((seq, part, state), BF16),
            pltpu.VMEM((seq, part, state), BF16),
            pltpu.VMEM((heads, 2 * HDIM, rows), F32),
            pltpu.VMEM((heads, 8, rows), F32),
            pltpu.VMEM((heads, HDIM, rows), BF16),
            pltpu.VMEM((heads, HDIM, rows), BF16),
            pltpu.VMEM((channels, rows), F32),
            pltpu.VMEM((rows, model), F32),
            pltpu.VMEM((owners, sub, model), BF16),
            pltpu.VMEM((owners, sub, model), BF16),
            pltpu.VMEM((owners, cap, gauss_width), BF16),
            dma((11,)),
            dma((heads,)),
            dma((heads,)),
            dma((heads,)),
            dma((heads,)),
            dma((heads, members)),
            dma((heads, members)),
            dma((seq,)),
            dma((seq,)),
            dma((seq,)),
            dma((seq,)),
            dma((heads,)),
            dma((heads,)),
            dma((owners,)),
            dma((owners,)),
            dma((owners,)),
            dma((owners,)),
        ],
        compiler_params=pltpu.CompilerParams(
            collective_id=0, has_side_effects=True, vmem_limit_bytes=56 * 1024 * 1024
        ),
    )(tokens, queries, key_rows, values, ssm_input, write_proj, read_proj, log_decay,
      attn_project, ssm_project, gauss_project, tile_owner.reshape(1, rows))


def solution(mesh):
    in_specs = (
        P("seq", None),
        P("seq", "head"),
        P("seq", "head"),
        P("seq", "head"),
        P("seq", "head"),
        P("seq", None),
        P("seq", None),
        P("head", "seq"),
        P("head", None),
        P("head", None),
        P(),
        P("seq"),
    )
    out_specs = (P(("seq", "head"), None), P("seq", "head", None, None, None))
    return jax.shard_map(
        functools.partial(per_device, mesh.shape["seq"], mesh.shape["head"]),
        mesh=mesh,
        in_specs=in_specs,
        out_specs=out_specs,
        check_vma=False,
    )
```

time: 195 us -> 46.7 us (0.24)
  waiting for transfers between devices: 100 us -> 0 us
  Pallas kernels: 0 us -> 42.7 us
  blocking collectives: 30.8 us -> 0 us
  local copies, waits for them, and re-layouts: 20.3 us -> 3.18 us
  matrix products: 16.2 us -> 0 us
  between operations: 14.5 us -> 0.64 us
  other arithmetic: 11.9 us -> 0 us
    all_gather x3 -> x0, waiting for transfers between devices: 79.8 us -> none  [the longest x1 40.5 us: fold_keys(): value_piece = lax.all_gather(values, 'seq', axis=0, tiled=True)]
    pallas_call x0 -> x1, Pallas kernels: none -> 42.7 us  [per_device(): pl.pallas_call(functools.partial(kernel, seq, owners), out_shape=(jax.Sha...]
    unnamed x1 -> x0, blocking collectives: 23.1 us -> none
    reduce_scatter x1 -> x0, waiting for transfers between devices: 20.3 us -> none  [per_device(): lax.psum_scatter((jnp.dot(attended, attn_project, preferred_element_type=...]
    dot_general x12 -> x0, matrix products: 16.2 us -> none  [the longest x2 5.39 us: one_step(): jnp.einsum('qhd,khd->hqk', query_heads, key_block, preferred_element_type...]
    dynamic_slice x19 -> x0, local copies, waits for them, and re-layouts: 11.5 us -> none  [the longest x16 8.8 us: hop(): part[k].astype(own.dtype)]
    all_to_all x1 -> x0, blocking collectives: 7.7 us -> none  [per_device(): lax.all_to_all(packed, 'head', split_axis=0, concat_axis=0, tiled=True)]
    reduce_sum x2 -> x0, other arithmetic: 6.06 us -> none  [one_step(): run_sum = run_sum * shrink + jnp.sum(raised, axis=2)]
  transfers between devices with their start and end apart: 4 -> 0, of which waited for: 4 -> 0; matrix products, arithmetic and copies ran while one was open for 11% -> 0% of each run, Pallas kernels for 0% -> 0%
where the time goes in v1:
time: 46.7 us; the launch traced here: 46.5 us
  Pallas kernels  42.7 us (91%)
  local copies, waits for them, and re-layouts  3.18 us (7%)
  between operations  0.64 us (1%)
    pallas_call x1, Pallas kernels, per_device(): pl.pallas_call(functools.partial(kernel, seq, owners), out_shape=(jax.Sha...  42.7 us
    unnamed x2, local copies, waits for them, and re-layouts  3.18 us

profile of v1, /device:TPU:0, one launch (start us, length us, event | category | flops | bytes accessed | tf_op | source)
XLA Modules:
  0.0 46.5 jit_solution(2701451371787310237)
XLA Ops:
  0.6 42.7 %shard_map.131 = (bf16[64,1024]{1,0:T(8,128)(2,1)}, bf16[1,1,4,32,768]{4,3,2,1,0:T(8,128)(2,1)}) custom-call(bf16[256,1024]{1,0:T(8,128)(2,1)} %tokens_hbm.1, bf16[256,256]{1,0:T(8,128)(2,1)} %queries_hbm.1, bf16[256,256]{1,0:T(8,128)(2,1)} %keys_hbm.1, bf16[256,256]{1,0:T(8,128)(2,1)} %values_hbm.1, bf16[256,512]{1,0:T(8,128)(2,1)} %ssm_hbm.1, ...), custom_call_target="tpu_custom_call" | custom-call | tf_op jit(solution)/shard_map/pallas_call | solution.py:398
  43.3 1.6 %copy.16 = bf16[64,1024]{1,0:T(8,128)(2,1)} copy(bf16[64,1024]{1,0:T(8,128)(2,1)} %get-tuple-element.4) | data formatting | bytes 262144
  44.9 1.6 %copy.17 = bf16[1,1,4,32,768]{4,3,2,1,0:T(8,128)(2,1)} copy(bf16[1,1,4,32,768]{4,3,2,1,0:T(8,128)(2,1)} %get-tuple-element.5) | data formatting | bytes 393216

commit v2 on v1

--- a/solution.py
+++ b/solution.py
@@ -75,13 +75,16 @@
     acc,
     top,
     o_out,
-    mix,
+    o_in,
     inner,
-    upd,
     up_out,
     up_in,
+    block_v,
     pk_out,
     load_sem,
+    out_sem,
+    wt_ss,
+    wt_rs,
     kv_ss,
     kv_rs,
     q_ss,
@@ -112,11 +115,15 @@
     sub = rows // owners
     cap = sub // 2
 
+    started = []
+
     def remote(src, dst, send, recv, target):
-        return pltpu.make_async_remote_copy(
+        copy = pltpu.make_async_remote_copy(
             src_ref=src, dst_ref=dst, send_sem=send, recv_sem=recv,
             device_id=target, device_id_type=MESH,
         )
+        started.append(copy)
+        return copy
 
     sources = [
         (queries_hbm, queries_v),
@@ -127,7 +134,7 @@
         (write_hbm, write_v),
         (read_hbm, read_v),
         (ssm_w_hbm, ssm_w),
-        (attn_w_hbm, attn_w),
+        (attn_w_hbm, attn_w.at[own]),
         (tokens_hbm.at[pl.ds(own * sub, sub)], tokens_v),
         (gauss_w_hbm, gauss_w),
     ]
@@ -139,9 +146,12 @@
     for r in range(1, seq):
         pl.semaphore_signal(barrier, inc=1, device_id={"seq": (me + r) % seq}, device_id_type=MESH)
     for r in range(1, owners):
-        pl.semaphore_signal(
-            barrier, inc=1, device_id={"head": (own + r) % owners}, device_id_type=MESH
-        )
+        for step in range(heads):
+            target = {
+                "seq": partner(my_head, step) * members + my_group,
+                "head": partner(own, r),
+            }
+            pl.semaphore_signal(barrier, inc=1, device_id=target, device_id_type=MESH)
 
     loads[0].wait()
     q_t = (queries_v[...].astype(F32) * (1.0 / math.sqrt(HDIM))).astype(BF16).T
@@ -152,7 +162,7 @@
     for h in range(heads):
         cols = slice(h * HDIM, (h + 1) * HDIM)
         kv_out[h] = jnp.concatenate([keys_v[:, cols], values_v[:, cols]], axis=1)
-    pl.semaphore_wait(barrier, seq - 1 + owners - 1)
+    pl.semaphore_wait(barrier, seq - 1 + (owners - 1) * heads)
 
     q_copies, kv_copies = [], []
     for r in range(1, heads):
@@ -178,6 +188,14 @@
         copy.start()
     forwards = {0: forward(0)}
     for copy in kv_copies:
+        copy.start()
+    loads[8].wait()
+    far = partner(own, 2)
+    wt_copies = [
+        remote(attn_w.at[own], attn_w.at[own], wt_ss.at[r], wt_rs.at[r], {"head": partner(own, r)})
+        for r in (2, 1)
+    ]
+    for copy in wt_copies:
         copy.start()
     q_in[my_head] = q_out[my_head]
     kv_in[me] = kv_out[my_head]
@@ -234,9 +252,62 @@
         mixing = (jnp.exp(jnp.where(causal, gaps, -jnp.inf)) * cross).astype(BF16)
         inner[g * width : (g + 1) * width] = dot(ssm_t[g * width : (g + 1) * width], mixing)
 
-    for r in range(1, heads):
+    key_rows = members * rows
+    below = lax.broadcasted_iota(jnp.int32, (2 * HDIM, key_rows), 0) < HDIM
+    zeros = jnp.zeros((HDIM, rows), BF16)
+    o_copies = []
+
+    def attend(r):
+        for m in range(1, members):
+            forwards[r][m - 1].wait_recv()
+        a = partner(my_head, r)
+        kv = kv_in[pl.ds(a * members, members)].reshape(key_rows, 2 * HDIM)
+        v_t = jnp.where(below, jnp.ones((), BF16), kv.T)
+        for c in reversed(range(heads)):
+            j = partner(my_head, c)
+            scores = dot(kv, jnp.concatenate([q_in[j], zeros], axis=0))
+            highest = jnp.max(scores, axis=0, keepdims=True)
+            if r:
+                before = top[c, 0:1]
+                highest = jnp.maximum(highest, before)
+            weights = jnp.exp(scores - highest).astype(BF16)
+            summed = dot(v_t, weights)
+            if r:
+                summed = summed + acc[c] * jnp.exp(before - highest)
+            if r < heads - 1:
+                acc[c] = summed
+                top[c] = jnp.broadcast_to(highest, (8, rows))
+                continue
+            head_out = summed[HDIM:] / summed[0:1]
+            for q in range(owners):
+                piece = head_out[:, q * sub : (q + 1) * sub]
+                o_out[c, q] = jnp.concatenate(
+                    [piece[: HDIM // 2], piece[HDIM // 2 :]], axis=1
+                ).astype(BF16)
+            slot = own * heads + my_head
+            for step in reversed(range(owners)):
+                q = partner(own, step)
+                if c == 0 and step == 0:
+                    o_in[slot] = o_out[c, q]
+                    continue
+                copy = remote(
+                    o_out.at[c, q], o_in.at[slot], o_ss.at[c, step], o_rs.at[c, step],
+                    {"seq": j * members + my_group, "head": q},
+                )
+                copy.start()
+                o_copies.append(copy)
+
+    def relay(r):
         kv_copies[r - 1].wait_recv()
         forwards[r] = forward(r)
+
+    for copy in q_copies:
+        copy.wait_recv()
+    attend(0)
+    relay(1)
+    relay(2)
+    attend(1)
+    relay(3)
 
     for copy in st_copies:
         copy.wait_recv()
@@ -257,44 +328,12 @@
         copy.start()
     en_in[me] = en_out[me]
 
-    for copy in q_copies:
-        copy.wait_recv()
-    key_rows = members * rows
-    below = lax.broadcasted_iota(jnp.int32, (2 * HDIM, key_rows), 0) < HDIM
-    zeros = jnp.zeros((HDIM, rows), BF16)
-    for r in range(heads):
-        for m in range(1, members):
-            forwards[r][m - 1].wait_recv()
-        a = partner(my_head, r)
-        kv = kv_in[pl.ds(a * members, members)].reshape(key_rows, 2 * HDIM)
-        v_t = jnp.where(below, jnp.ones((), BF16), kv.T)
-        for c in range(heads):
-            scores = dot(kv, jnp.concatenate([q_in[c], zeros], axis=0))
-            highest = jnp.max(scores, axis=0, keepdims=True)
-            if r:
-                before = top[c, 0:1]
-                highest = jnp.maximum(highest, before)
-            weights = jnp.exp(scores - highest).astype(BF16)
-            summed = dot(v_t, weights)
-            if r:
-                summed = summed + acc[c] * jnp.exp(before - highest)
-            if r < heads - 1:
-                acc[c] = summed
-                top[c] = jnp.broadcast_to(highest, (8, rows))
-            else:
-                o_out[c] = (summed[HDIM:] / summed[0:1]).astype(BF16)
-    o_copies = []
-    for r in range(1, heads):
-        j = partner(my_head, r)
-        o_copies.append(
-            remote(
-                o_out.at[j], mix.at[my_head], o_ss.at[r], o_rs.at[r],
-                {"seq": j * members + my_group},
-            )
-        )
-    for copy in o_copies:
-        copy.start()
-    mix[my_head] = o_out[my_head]
+    wt_copies[0].wait_recv()
+    wt_relay = remote(
+        attn_w.at[far], attn_w.at[far], wt_ss.at[3], wt_rs.at[3], {"head": partner(own, 1)}
+    )
+    wt_relay.start()
+    attend(2)
 
     for copy in en_copies:
         copy.wait_recv()
@@ -311,7 +350,17 @@
         mean = jnp.mean(out * out, axis=0, keepdims=True)
         mixed.append((out * lax.rsqrt(mean + 1e-05)).astype(BF16))
     loads[7].wait()
-    upd[...] = dot_tn(jnp.concatenate(mixed, axis=0), ssm_w[...])
+    update = dot_tn(jnp.concatenate(mixed, axis=0), ssm_w[...])
+    for q in range(owners):
+        up_out[q] = update[q * sub : (q + 1) * sub].astype(BF16)
+    up_copies = []
+    for r in (3, 2, 1):
+        q = partner(own, r)
+        up_copies.append(
+            remote(up_out.at[q], up_in.at[r], up_ss.at[r], up_rs.at[r], {"head": q})
+        )
+    for copy in up_copies:
+        copy.start()
 
     named = jnp.zeros((1, sub), jnp.int32)
     for q in range(owners):
@@ -332,21 +381,7 @@
         lax.broadcasted_iota(jnp.int32, (owners * cap, sub), 0) == slot, 1.0, 0.0
     ).astype(BF16)
 
-    loads[8].wait()
-    for copy in o_copies:
-        copy.wait_recv()
-    attended = mix[...].reshape(heads * HDIM, rows)
-    update = upd[...] + dot_tn(attended, attn_w[...])
-    for q in range(owners):
-        up_out[q] = update[q * sub : (q + 1) * sub].astype(BF16)
-    up_copies = []
-    for r in (3, 2, 1) if owners == 4 else range(1, owners):
-        q = partner(own, r)
-        up_copies.append(
-            remote(up_out.at[q], up_in.at[r], up_ss.at[r], up_rs.at[r], {"head": q})
-        )
-    for copy in up_copies:
-        copy.start()
+    attend(3)
     loads[9].wait()
     loads[10].wait()
     summed = up_out[own].astype(F32)
@@ -354,27 +389,48 @@
         copy.wait_recv()
     for r in range(1, owners):
         summed = summed + up_in[r].astype(F32)
+    wt_copies[1].wait_recv()
+    wt_relay.wait_recv()
+    for copy in o_copies:
+        copy.wait_recv()
+    halves = o_in[...]
+    attended = jnp.concatenate([halves[:, :, :sub], halves[:, :, sub:]], axis=1)
+    attended = attended.reshape(owners * heads * HDIM, sub)
+    summed = summed + dot_tn(attended, attn_w[...].reshape(owners * heads * HDIM, summed.shape[1]))
     block = (tokens_v[...].astype(F32) + summed).astype(BF16)
-    block_out[...] = block
+    block_v[...] = block
+    block_copy = pltpu.make_async_copy(block_v, block_out, out_sem.at[0])
+    block_copy.start()
     gauss = dot(block, gauss_w[...]).astype(BF16)
     packed = dot(selector, gauss).astype(BF16)
     for q in range(owners):
         pk_out[q] = packed[q * cap : (q + 1) * cap]
     tl_copies = []
-    for r in (3, 2, 1) if owners == 4 else range(1, owners):
+    for r in (3, 2, 1):
         q = partner(own, r)
         tl_copies.append(
             remote(pk_out.at[q], tiles_out.at[0, 0, own], tl_ss.at[r], tl_rs.at[r], {"head": q})
         )
     for copy in tl_copies:
         copy.start()
-    tiles_out[0, 0, own] = pk_out[own]
-    for copy in q_copies + kv_copies + st_copies + en_copies + o_copies + up_copies:
+    tile_copy = pltpu.make_async_copy(pk_out.at[own], tiles_out.at[0, 0, own], out_sem.at[1])
+    tile_copy.start()
+    for copy in tl_copies:
+        copy.wait_recv()
+    block_copy.wait()
+    tile_copy.wait()
+    for copy in started:
         copy.wait_send()
-    for copies in forwards.values():
-        for copy in copies:
-            copy.wait_send()
-    for copy in tl_copies:
+
+
+def hand_over(block_in, tiles_in, block_out, tiles_out, sem):
+    copies = [
+        pltpu.make_async_copy(block_in, block_out, sem.at[0]),
+        pltpu.make_async_copy(tiles_in, tiles_out, sem.at[1]),
+    ]
+    for copy in copies:
+        copy.start()
+    for copy in copies:
         copy.wait()
 
 
@@ -395,14 +451,15 @@
     vmem = pl.BlockSpec(memory_space=pltpu.VMEM)
     dma = pltpu.SemaphoreType.DMA
     like = lambda a: pltpu.VMEM(a.shape, a.dtype)
-    return pl.pallas_call(
+    shapes = (
+        jax.ShapeDtypeStruct((sub, model), BF16),
+        jax.ShapeDtypeStruct((1, 1, owners, cap, gauss_width), BF16),
+    )
+    results = pl.pallas_call(
         functools.partial(kernel, seq, owners),
-        out_shape=(
-            jax.ShapeDtypeStruct((sub, model), BF16),
-            jax.ShapeDtypeStruct((1, 1, owners, cap, gauss_width), BF16),
-        ),
+        out_shape=shapes,
         in_specs=[hbm] * 11 + [vmem],
-        out_specs=(vmem, vmem),
+        out_specs=(hbm, hbm),
         scratch_shapes=[
             pltpu.VMEM((sub, model), BF16),
             like(queries),
@@ -412,7 +469,7 @@
             like(write_proj),
             like(read_proj),
             like(log_decay),
-            like(attn_project),
+            pltpu.VMEM((owners, *attn_project.shape), BF16),
             like(ssm_project),
             like(gauss_project),
             pltpu.VMEM((heads, rows, 2 * HDIM), BF16),
@@ -425,14 +482,17 @@
             pltpu.VMEM((seq, part, state), BF16),
             pltpu.VMEM((heads, 2 * HDIM, rows), F32),
             pltpu.VMEM((heads, 8, rows), F32),
-            pltpu.VMEM((heads, HDIM, rows), BF16),
-            pltpu.VMEM((heads, HDIM, rows), BF16),
+            pltpu.VMEM((heads, owners, HDIM // 2, 2 * sub), BF16),
+            pltpu.VMEM((owners * heads, HDIM // 2, 2 * sub), BF16),
             pltpu.VMEM((channels, rows), F32),
-            pltpu.VMEM((rows, model), F32),
             pltpu.VMEM((owners, sub, model), BF16),
             pltpu.VMEM((owners, sub, model), BF16),
+            pltpu.VMEM((sub, model), BF16),
             pltpu.VMEM((owners, cap, gauss_width), BF16),
             dma((11,)),
+            dma((2,)),
+            dma((owners,)),
+            dma((owners,)),
             dma((heads,)),
             dma((heads,)),
             dma((heads,)),
@@ -443,8 +503,8 @@
             dma((seq,)),
             dma((seq,)),
             dma((seq,)),
-            dma((heads,)),
-            dma((heads,)),
+            dma((heads, owners)),
+            dma((heads, owners)),
             dma((owners,)),
             dma((owners,)),
             dma((owners,)),
@@ -455,6 +515,13 @@
         ),
     )(tokens, queries, key_rows, values, ssm_input, write_proj, read_proj, log_decay,
       attn_project, ssm_project, gauss_project, tile_owner.reshape(1, rows))
+    return pl.pallas_call(
+        hand_over,
+        out_shape=shapes,
+        in_specs=[hbm, hbm],
+        out_specs=(hbm, hbm),
+        scratch_shapes=[dma((2,))],
+    )(*results)
 
 
 def solution(mesh):

time: 46.7 us -> 52.1 us (1.12)
  Pallas kernels: 42.7 us -> 51.3 us
  local copies, waits for them, and re-layouts: 3.18 us -> 0 us
    pallas_call x1 -> x2, Pallas kernels: 42.7 us -> 51.3 us  [the longest x1 40.3 us: per_device(): pl.pallas_call(functools.partial(kernel, seq, owners), out_shape=shapes,...]
    unnamed x2 -> x0, local copies, waits for them, and re-layouts: 3.18 us -> none
where the time goes in v2:
time: 52.1 us; the launch traced here: 52 us
  Pallas kernels  51.3 us (98%)
  between operations  0.64 us (1%)
    pallas_call x1, Pallas kernels, per_device(): pl.pallas_call(functools.partial(kernel, seq, owners), out_shape=shapes,...  40.3 us
    pallas_call x1, Pallas kernels, per_device(): pl.pallas_call(hand_over, out_shape=shapes, in_specs=[hbm, hbm], out_spec...  11 us

profile of v2, /device:TPU:0, one launch (start us, length us, event | category | flops | bytes accessed | tf_op | source)
XLA Modules:
  0.0 52.0 jit_solution(16816147136252728146)
XLA Ops:
  0.6 40.3 %shard_map.131 = (bf16[64,1024]{1,0:T(8,128)(2,1)}, bf16[1,1,4,32,768]{4,3,2,1,0:T(8,128)(2,1)}) custom-call(bf16[256,1024]{1,0:T(8,128)(2,1)} %tokens_hbm.1, bf16[256,256]{1,0:T(8,128)(2,1)} %queries_hbm.1, bf16[256,256]{1,0:T(8,128)(2,1)} %keys_hbm.1, bf16[256,256]{1,0:T(8,128)(2,1)} %values_hbm.1, bf16[256,512]{1,0:T(8,128)(2,1)} %ssm_hbm.1, ...), custom_call_target="tpu_custom_call" | custom-call | tf_op jit(solution)/shard_map/pallas_call | solution.py:458
  40.9 11.0 %shard_map.132 = (bf16[64,1024]{1,0:T(8,128)(2,1)}, bf16[1,1,4,32,768]{4,3,2,1,0:T(8,128)(2,1)}) custom-call(bf16[64,1024]{1,0:T(8,128)(2,1)} %get-tuple-element.4.block_in, bf16[1,1,4,32,768]{4,3,2,1,0:T(8,128)(2,1)} %get-tuple-element.5.tiles_in), custom_call_target="tpu_custom_call" | custom-call | tf_op jit(solution)/shard_map/pallas_call | solution.py:518
